TPU v7x, 256 devices: a whole 4x4x8 slice. The times are simulated.
256 devices in a mesh: row: 8 (over z), col: 32 (over y, x, core).
Axes of the slice: x: 4, y: 4, z: 8, core: 2. Of those that a mesh axis runs over, the one named last changes fastest.
Arguments:
- matrix: float32 [12288, 12288], P('row', 'col'), may hold values from -160 to 160, as said below
- pattern: int32 [32, 32], replicated, may hold values from 0 to 1, as said below
- row_order: int32 [32], replicated, may hold values from 0 to 31, as said below
- col_order: int32 [32], replicated, may hold values from 0 to 31, as said below
Outputs:
- factored: float32 [12288, 12288], P('row', 'col')
Inputs may be any that keep to these rules, and one draw needn't show every extreme that they name: `row_order`: a permutation of 0 to 31. `col_order`: a permutation of 0 to 31. Symmetric with ones on the diagonal; pattern[1, 0] = 1; pattern[I, J] = 1 whenever pattern[I, 0] = pattern[J, 0] = 1, and whenever pattern[I, 1] = pattern[J, 1] = 1 with I, J >= 1. `matrix`: read in natural block order the window is symmetric, and its retained lower blocks make the pivot block of supernode 0, and that of supernode 1 after the first update, positive definite.
All inputs are finite; a program needn't handle non-finite values.
Results may differ from a plain program's by a relative error of at most 0.0003.
Values sent between devices are 32-bit elements; how exact they have to be, the bound alone decides.
A program may use at most 128 MiB of HBM per device.

v0:
```python
import jax
import jax.numpy as jnp
from jax import lax
from jax.sharding import PartitionSpec as P

BLOCK = 384


def broadcast(value, axis, root):
    return lax.dynamic_index_in_dim(lax.all_gather(value, axis), root, 0, keepdims=False)


def cut_along(value, dim, devices):
    lengths = value.shape
    blocks = value.reshape(*lengths[:dim], devices, lengths[dim] // devices, *lengths[dim + 1 :])
    return jnp.moveaxis(blocks, dim, 0)


def summed_on_arrival(value, axis, dim):
    blocks = cut_along(value, dim, lax.axis_size(axis))
    arrived = lax.all_to_all(blocks, axis, split_axis=0, concat_axis=0, tiled=True)
    return arrived.sum(axis=0)


def sent_to_all(value, axis):
    devices = lax.axis_size(axis)
    return lax.all_to_all(
        jnp.broadcast_to(value[None], (devices, *value.shape)), axis, 0, 0, tiled=True
    )


def in_order(blocks, dim):
    lengths = list(blocks.shape[1:])
    lengths[dim] *= blocks.shape[0]
    return jnp.moveaxis(blocks, 0, dim).reshape(lengths)


def collect(value, axis, dim):
    blocks = sent_to_all(value, axis)
    return in_order(blocks, dim)


def positions(order):
    indices = jnp.arange(order.shape[0], dtype=jnp.int32)
    return jnp.sum(jnp.where(order[None, :] == indices[:, None], indices[None, :], 0), axis=1)


def look_up(table, wanted):
    indices = jnp.arange(table.shape[0], dtype=jnp.int32)
    return jnp.sum(jnp.where(indices[None, :] == wanted[:, None], table[None, :], 0), axis=1)


def expand(flags, tall, broad):
    return jnp.repeat(jnp.repeat(flags, tall, axis=0), broad, axis=1)


def body(matrix, pattern, row_order, col_order):
    local_rows, width = matrix.shape
    total = row_order.shape[0]
    blocks_here = local_rows // BLOCK
    piece_width = min(width, BLOCK)
    piece_count = width // piece_width
    share_rows = local_rows // lax.axis_size("col")
    row_here = lax.axis_index("row")
    col_here = lax.axis_index("col")
    row_place = positions(row_order)
    col_place = positions(col_order)
    indices = jnp.arange(total, dtype=jnp.int32)
    stored_rows = row_here * blocks_here + jnp.arange(blocks_here, dtype=jnp.int32)
    row_ids = look_up(row_order, stored_rows)
    starts = col_here * width + piece_width * jnp.arange(piece_count, dtype=jnp.int32)
    col_ids = look_up(col_order, starts // BLOCK)
    offsets = starts % BLOCK
    row_select = (row_ids[:, None] == indices[None, :]).astype(jnp.int32)
    col_select = (col_ids[:, None] == indices[None, :]).astype(jnp.int32)
    marked = jnp.dot(jnp.dot(row_select, pattern), col_select.T)
    lower = row_ids[:, None] >= col_ids[None, :]
    retain = expand((marked == 1) & lower, BLOCK, piece_width).astype(jnp.float32)
    lower_full = expand(lower, BLOCK, piece_width).astype(jnp.float32)
    current = matrix * retain
    identity = jnp.eye(BLOCK, dtype=jnp.float32)
    for supernode in range(2):
        wanted = jnp.full((1,), supernode, jnp.int32)
        center = look_up(row_place, wanted)[0]
        root_row = center // blocks_here
        center_local = center % blocks_here
        column_start = look_up(col_place, wanted)[0] * BLOCK
        in_column = look_up(pattern[:, supernode], row_ids)
        struct_rows = ((in_column == 1) & (row_ids > supernode)).astype(jnp.float32)
        used_rows = jnp.repeat(struct_rows, BLOCK)
        anchor = column_start + 0
        section = lax.dynamic_slice(
            current, (center_local * BLOCK, anchor % width), (BLOCK, piece_width)
        )
        center_parts = broadcast(section, "col", anchor // width)
        holding = (col_here * width // BLOCK == column_start // BLOCK).astype(jnp.float32)
        embedded = current * holding
        own_rows = summed_on_arrival(embedded, "col", 0)
        pivot_values = broadcast(center_parts, "row", root_row)
        factor = jnp.linalg.cholesky(pivot_values)
        inverse = jax.scipy.linalg.solve_triangular(factor, identity, lower=True)
        share_mask = lax.dynamic_slice_in_dim(used_rows, col_here * share_rows, share_rows, 0)
        part_scaled = jnp.dot(
            own_rows * share_mask[:, None], inverse.T, precision=lax.Precision.HIGHEST
        )
        scaled = collect(part_scaled, "col", 0)
        column_piece = 0
        holder = look_up(row_place, col_ids)[0]
        section = lax.dynamic_slice_in_dim(
            scaled, holder % blocks_here * BLOCK + offsets[column_piece], piece_width, 0
        )
        fetched = broadcast(section, "row", holder // blocks_here)
        update = jnp.dot(scaled, fetched.T, precision=lax.Precision.HIGHEST)
        current = current - update * lower_full
        is_center = jnp.repeat(row_ids == supernode, BLOCK)
        column = jnp.where(is_center[:, None], jnp.tile(factor, (blocks_here, 1)), scaled)
        column_piece = 0
        present = current
        replaced = jnp.where(col_ids[column_piece] == supernode, column, present)
        current = replaced
    return current * retain


def solution(mesh):
    in_specs = (P("row", "col"), P(), P(), P())
    out_specs = P("row", "col")
    return jax.shard_map(body, mesh=mesh, in_specs=in_specs, out_specs=out_specs, check_vma=False)
```

profile of v0, /device:TPU:1, one launch (start us, length us, event | category | flops | bytes accessed | tf_op | source)
XLA Modules:
  0.0 730.2 jit_solution(2760003659194418651)
XLA Ops:
  15.9 3.4 broadcast_multiply_fusion.1
  21.7 86.9 %all-gather.15.cloned.1.call-done = f32[12288,384]{1,0:T(8,128)} async-done(((f32[384,384]{1,0:T(8,128)}), f32[12288,384]{1,0:T(8,128)}) %all-gather.15.cloned.1.call-update) | async-done | bytes 18874384 | tf_op jit(solution)/shard_map/all_gather | solution.py:10
  108.6 1.9 constant_dynamic-slice_fusion.8
  110.5 5.4 all-to-all-start
  118.9 27.7 %all-to-all-done = f32[32,48,384]{2,1,0:T(8,128)S(1)} async-done(((f32[32,48,384]{2,1,0:T(8,128)}), f32[32,48,384]{2,1,0:T(8,128)S(1)}, u32[]{:S(2)}, u32[]{:S(2)}) %all-to-all-start) | async-done | bytes 2359328 | tf_op jit(solution)/shard_map/all_to_all | solution.py:21
  147.4 22.1 %all-gather.11.cloned.1.call-done = f32[8,384,384]{2,1,0:T(8,128)} async-done(((f32[1,384,384]{2,1,0:T(8,128)}), f32[8,384,384]{2,1,0:T(8,128)}) %all-gather.11.cloned.1.call-update) | async-done | bytes 4718608 | tf_op jit(solution)/shard_map/all_gather | solution.py:10
  172.0 11.7 %cholesky.208 = f32[128,128]{1,0:T(8,128)S(1)} custom-call(f32[128,128]{1,0:T(8,128)S(1)} %cholesky.310), custom_call_target="Cholesky" | custom-call | tf_op jit(solution)/shard_map/jit(cholesky)/cholesky | solution.py:100
  184.5 9.8 %custom-call.20 = f32[1,128,128]{1,2,0:T(8,128)S(1)} custom-call(f32[1,128,128]{2,1,0:T(8,128)S(1)} %get-tuple-element.71), custom_call_target="InvertDiagBlocksLowerTriangular" | custom-call | tf_op jit(solution)/shard_map/jit(cholesky)/cholesky | solution.py:100
  194.9 11.7 %cholesky.227 = f32[128,128]{1,0:T(8,128)S(1)} custom-call(f32[128,128]{1,0:T(8,128)S(1)} %cholesky.314), custom_call_target="Cholesky" | custom-call | tf_op jit(solution)/shard_map/jit(cholesky)/cholesky | solution.py:100
  207.3 10.1 %custom-call.21 = f32[1,128,128]{1,2,0:T(8,128)S(1)} custom-call(f32[1,128,128]{2,1,0:T(8,128)S(1)} %get-tuple-element.68), custom_call_target="InvertDiagBlocksLowerTriangular" | custom-call | tf_op jit(solution)/shard_map/jit(cholesky)/cholesky | solution.py:100
  217.9 11.7 %cholesky.246 = f32[128,128]{1,0:T(8,128)S(1)} custom-call(f32[128,128]{1,0:T(8,128)S(1)} %convolution_subtract_fusion.7), custom_call_target="Cholesky" | custom-call | tf_op jit(solution)/shard_map/jit(cholesky)/cholesky | solution.py:100
  232.4 6.2 while.4
  238.6 29.5 %custom-call.22 = f32[3,128,128]{1,2,0:T(8,128)S(1)} custom-call(f32[3,128,128]{2,1,0:T(8,128)S(1)} %get-tuple-element.21), custom_call_target="InvertDiagBlocksLowerTriangular" | custom-call | tf_op jit(solution)/shard_map/jit(_solve_triangular)/triangular_solve | solution.py:101
  272.3 7.5 %all-to-all-start.1 = ((f32[32,48,384]{2,1,0:T(8,128)}), f32[32,48,384]{2,1,0:T(8,128)S(1)}, u32[]{:S(2)}, u32[]{:S(2)}) async-start(f32[32,48,384]{2,1,0:T(8,128)} %broadcast_in_dim.165), calls=%async_computation.1 | async-start | bytes 4718592 | tf_op jit(solution)/shard_map/all_to_all | solution.py:27
  281.7 28.8 %all-to-all-done.1 = f32[32,48,384]{2,1,0:T(8,128)S(1)} async-done(((f32[32,48,384]{2,1,0:T(8,128)}), f32[32,48,384]{2,1,0:T(8,128)S(1)}, u32[]{:S(2)}, u32[]{:S(2)}) %all-to-all-start.1) | async-done | bytes 2359328 | tf_op jit(solution)/shard_map/all_to_all | solution.py:27
  319.0 48.6 %all-gather.17.cloned.1.call-done = f32[3072,384]{1,0:T(8,128)} async-done(((f32[384,384]{1,0:T(8,128)}), f32[3072,384]{1,0:T(8,128)}) %all-gather.17.cloned.1.call-update) | async-done | bytes 4718608 | tf_op jit(solution)/shard_map/all_gather | solution.py:10
  367.6 7.3 %broadcast_multiply_fusion = (f32[1536,384]{1,0:T(8,128)}, f32[1536,384]{1,0:T(8,128)S(1)}) fusion(f32[]{:T(128)S(6)} %convert_element_type.27, f32[1536,384]{1,0:T(8,128)} %bitcast_select_fusion.1, f32[1536,384]{1,0:T(8,128)} %copy-done.1, f32[1536,384]{1,0:T(8,128)S(1)} %bitcast.128, f32[8,384,384]{2,1,0:T(8,128)} %bitcast.131, s32[]{:T(128)S(6)} %select_n.190, ...), kind=kOutput, calls=%fused_computation.13 | convolution fusion | flops 2720268288 | bytes 12387849 | tf_op jit(solution)/shard_map/dot_general | solution.py:113
  377.2 81.7 %all-gather.19.cloned.1.call-done = f32[12288,384]{1,0:T(8,128)} async-done(((f32[384,384]{1,0:T(8,128)}), f32[12288,384]{1,0:T(8,128)}) %all-gather.19.cloned.1.call-update) | async-done | bytes 18874384 | tf_op jit(solution)/shard_map/all_gather | solution.py:10
  458.9 1.9 constant_dynamic-slice_fusion.4
  460.8 5.4 all-to-all-start.2
  467.2 29.7 %all-to-all-done.2 = f32[32,48,384]{2,1,0:T(8,128)S(1)} async-done(((f32[32,48,384]{2,1,0:T(8,128)}), f32[32,48,384]{2,1,0:T(8,128)S(1)}, u32[]{:S(2)}, u32[]{:S(2)}) %all-to-all-start.2) | async-done | bytes 2359328 | tf_op jit(solution)/shard_map/all_to_all | solution.py:21
  497.7 22.1 %all-gather.13.cloned.1.call-done = f32[8,384,384]{2,1,0:T(8,128)} async-done(((f32[1,384,384]{2,1,0:T(8,128)}), f32[8,384,384]{2,1,0:T(8,128)}) %all-gather.13.cloned.1.call-update) | async-done | bytes 4718608 | tf_op jit(solution)/shard_map/all_gather | solution.py:10
  522.3 11.7 %cholesky.261 = f32[128,128]{1,0:T(8,128)S(1)} custom-call(f32[128,128]{1,0:T(8,128)S(1)} %cholesky.318), custom_call_target="Cholesky" | custom-call | tf_op jit(solution)/shard_map/jit(cholesky)/cholesky | solution.py:100
  534.8 9.8 %custom-call.23 = f32[1,128,128]{1,2,0:T(8,128)S(1)} custom-call(f32[1,128,128]{2,1,0:T(8,128)S(1)} %get-tuple-element.64), custom_call_target="InvertDiagBlocksLowerTriangular" | custom-call | tf_op jit(solution)/shard_map/jit(cholesky)/cholesky | solution.py:100
  545.2 11.7 %cholesky.280 = f32[128,128]{1,0:T(8,128)S(1)} custom-call(f32[128,128]{1,0:T(8,128)S(1)} %cholesky.322), custom_call_target="Cholesky" | custom-call | tf_op jit(solution)/shard_map/jit(cholesky)/cholesky | solution.py:100
  557.6 10.0 %custom-call.24 = f32[1,128,128]{1,2,0:T(8,128)S(1)} custom-call(f32[1,128,128]{2,1,0:T(8,128)S(1)} %get-tuple-element.61), custom_call_target="InvertDiagBlocksLowerTriangular" | custom-call | tf_op jit(solution)/shard_map/jit(cholesky)/cholesky | solution.py:100
  568.1 11.7 %cholesky.299 = f32[128,128]{1,0:T(8,128)S(1)} custom-call(f32[128,128]{1,0:T(8,128)S(1)} %convolution_subtract_fusion.6), custom_call_target="Cholesky" | custom-call | tf_op jit(solution)/shard_map/jit(cholesky)/cholesky | solution.py:100
  582.5 6.1 while.5
  588.7 29.5 %custom-call.25 = f32[3,128,128]{1,2,0:T(8,128)S(1)} custom-call(f32[3,128,128]{2,1,0:T(8,128)S(1)} %get-tuple-element.22), custom_call_target="InvertDiagBlocksLowerTriangular" | custom-call | tf_op jit(solution)/shard_map/jit(_solve_triangular)/triangular_solve | solution.py:101
  620.9 39.0 %all_to_all.20 = f32[32,48,384]{2,1,0:T(8,128)S(1)} all-to-all(f32[32,48,384]{2,1,0:T(8,128)S(1)} %broadcast_in_dim.171), channel_id=1, replica_groups=mesh['row'=8,'col'=32] {'col'}, dimensions={0} | all-to-all | bytes 4718592 | tf_op jit(solution)/shard_map/all_to_all | solution.py:27
  663.2 52.3 %all-gather.21.cloned.1.call-done = f32[3072,384]{1,0:T(8,128)} async-done(((f32[384,384]{1,0:T(8,128)}), f32[3072,384]{1,0:T(8,128)}) %all-gather.21.cloned.1.call-update) | async-done | bytes 4718608 | tf_op jit(solution)/shard_map/all_gather | solution.py:10
  715.5 7.5 %fusion.4 = f32[1536,384]{1,0:T(8,128)} fusion(f32[1536,384]{1,0:T(8,128)} %bitcast_select_fusion, f32[1536,384]{1,0:T(8,128)} %copy-done, f32[1536,384]{1,0:T(8,128)S(1)} %bitcast.126, f32[1536]{0:T(1024)S(1)} %convert_element_type.29, pred[1536]{0:T(1024)(128)(4,1)S(1)} %broadcast_in_dim.167, pred[]{:T(512)S(6)} %eq.173, f32[8,384,384]{2,1,0:T(8,128)} %bitcast.132, ...), kind=kOutput, calls=%fused_computation.10 | convolution fusion | flops 2720268288 | bytes 10034693 | tf_op jit(solution)/shard_map/dot_general | solution.py:113
  (132 shorter events, 53.5 us)
Async XLA Ops:
  6.5 102.1 %all-gather.15.cloned.1.call-start = ((), (), s32[]{:S(2)}) async-start(), calls=%async_computation.6 | async-start | bytes 19464192 | tf_op jit(solution)/shard_map/all_gather | solution.py:10
  19.4 1.4 copy-start.1
  21.7 147.9 %all-gather.11.cloned.1.call-start = ((), (), s32[]{:S(2)}) async-start(), calls=%async_computation.4 | async-start | bytes 5308416 | tf_op jit(solution)/shard_map/all_gather | solution.py:10
  110.5 6.1 copy-start.4
  110.5 36.1 %all-to-all-start = ((f32[32,48,384]{2,1,0:T(8,128)}), f32[32,48,384]{2,1,0:T(8,128)S(1)}, u32[]{:S(2)}, u32[]{:S(2)}) async-start(f32[32,48,384]{2,1,0:T(8,128)} %bitcast.129), calls=%async_computation | async-start | bytes 4718592 | tf_op jit(solution)/shard_map/all_to_all | solution.py:21
  172.0 60.3 %copy-start.7 = (s32[3]{0:T(128)S(1)}, s32[3]{0:T(128)}, u32[]{:S(2)}) copy-start(s32[3]{0:T(128)} %iota_multiply_fusion) | copy-start | bytes 40
  232.3 37.6 %copy-start.3 = (f32[48,384]{1,0:T(8,128)S(1)}, f32[48,384]{1,0:T(8,128)}, u32[]{:S(2)}) copy-start(f32[48,384]{1,0:T(8,128)} %reduce_sum.127) | copy-start | bytes 221188
  272.3 38.3 %all-to-all-start.1 = ((f32[32,48,384]{2,1,0:T(8,128)}), f32[32,48,384]{2,1,0:T(8,128)S(1)}, u32[]{:S(2)}, u32[]{:S(2)}) async-start(f32[32,48,384]{2,1,0:T(8,128)} %broadcast_in_dim.165), calls=%async_computation.1 | async-start | bytes 4718592 | tf_op jit(solution)/shard_map/all_to_all | solution.py:27
  279.8 87.8 %all-gather.17.cloned.1.call-start = ((), (), s32[]{:S(2)}) async-start(), calls=%async_computation.7 | async-start | bytes 5308416 | tf_op jit(solution)/shard_map/all_gather | solution.py:10
  311.5 147.4 %all-gather.19.cloned.1.call-start = ((), (), s32[]{:S(2)}) async-start(), calls=%async_computation.8 | async-start | bytes 19464192 | tf_op jit(solution)/shard_map/all_gather | solution.py:10
  374.9 1.4 copy-start
  377.1 142.7 %all-gather.13.cloned.1.call-start = ((), (), s32[]{:S(2)}) async-start(), calls=%async_computation.5 | async-start | bytes 5308416 | tf_op jit(solution)/shard_map/all_gather | solution.py:10
  460.8 6.3 copy-start.6
  460.8 36.1 %all-to-all-start.2 = ((f32[32,48,384]{2,1,0:T(8,128)}), f32[32,48,384]{2,1,0:T(8,128)S(1)}, u32[]{:S(2)}, u32[]{:S(2)}) async-start(f32[32,48,384]{2,1,0:T(8,128)} %bitcast.130), calls=%async_computation.2 | async-start | bytes 4718592 | tf_op jit(solution)/shard_map/all_to_all | solution.py:21
  466.2 249.3 %all-gather.21.cloned.1.call-start = ((), (), s32[]{:S(2)}) async-start(), calls=%async_computation.9 | async-start | bytes 5308416 | tf_op jit(solution)/shard_map/all_gather | solution.py:10
  582.5 37.5 %copy-start.2 = (f32[48,384]{1,0:T(8,128)S(1)}, f32[48,384]{1,0:T(8,128)}, u32[]{:S(2)}) copy-start(f32[48,384]{1,0:T(8,128)} %reduce_sum.132) | copy-start | bytes 221188
  620.9 40.5 %copy-start.5 = (pred[4]{0:T(512)(128)(4,1)S(1)}, pred[4]{0:T(512)(128)(4,1)}, u32[]{:S(2)}) copy-start(pred[4]{0:T(512)(128)(4,1)} %get-tuple-element.76) | copy-start | bytes 16
Sparse Core Ops, SparseCore 0:
  21.8 86.7 all-gather.14
  110.7 58.8 all-gather.10
  311.6 55.9 all-gather.16
  377.3 81.5 all-gather.18
  460.9 58.8 all-gather.12
  660.9 54.5 all-gather.20
where the time goes:
time: 741 us; the launch traced here: 730 us
  waiting for transfers between devices  400 us (54%)
  other arithmetic  191 us (26%)
  blocking collectives  39 us (5%)
  local copies, waits for them, and re-layouts  29.6 us (4%)
  between operations  28.4 us (4%)
  matrix products  23.5 us (3%)
  starting transfers between devices  18.7 us (3%)
    all_gather x6, waiting for transfers between devices, broadcast(): lax.all_gather(value, axis)  314 us
    another operation x22, other arithmetic, body(): factor = jnp.linalg.cholesky(pivot_values)  114 us
    another operation x5, other arithmetic, body(): inverse = jax.scipy.linalg.solve_triangular(factor, identity, lower=True)  59.7 us
    all_to_all x2, waiting for transfers between devices, summed_on_arrival(): lax.all_to_all(blocks, axis, split_axis=0, concat_axis=0, tiled=True)  57.5 us
    all_to_all x1, blocking collectives, sent_to_all(): lax.all_to_all(jnp.broadcast_to(value[None], (devices, *value.shape)), ax...  39 us
    all_to_all x1, waiting for transfers between devices, sent_to_all(): lax.all_to_all(jnp.broadcast_to(value[None], (devices, *value.shape)), ax...  28.8 us
  transfers between devices with their start and end apart: 9, of which 9 were waited for; matrix products, arithmetic and copies ran while one was open for 1% of the time, Pallas kernels for 0%

commit v1 on v0

v1 whole, which is shorter than its diff:
```python
import jax
import jax.numpy as jnp
from jax import lax
from jax.experimental import pallas as pl
from jax.experimental.pallas import tpu as pltpu
from jax.sharding import PartitionSpec as P

BLOCK = 384
TILE = 128
CHUNK = BLOCK // 16
SHARE = BLOCK // 8
MESH = pl.DeviceIdType.MESH
EXACT = lax.Precision.HIGHEST
F32 = jnp.float32
BF16 = jnp.bfloat16
ROWS_COLS = ((1,), (0,))
COLS_COLS = ((0,), (0,))
ROWS_ROWS = ((1,), (1,))


def product(left, right, over):
    return lax.dot_general(
        left, right, (over, ((), ())), precision=EXACT, preferred_element_type=F32
    )


def split(value):
    high = value.astype(BF16)
    return high, (value - high.astype(F32)).astype(BF16)


def product3(left, right, over):
    def part(a, b):
        return lax.dot_general(a, b, (over, ((), ())), preferred_element_type=F32)

    return part(left[0], right[0]) + (part(left[0], right[1]) + part(left[1], right[0]))


def lane(value, k):
    return jnp.broadcast_to(value[:, k : k + 1], (8, TILE))


def sublane(value, k):
    return jnp.broadcast_to(value[k : k + 1, :], (8, TILE))


def tree(terms):
    while len(terms) > 1:
        terms = [terms[i] + terms[i + 1] for i in range(0, len(terms), 2)]
    return terms[0]


def factor_tile(rows):
    lanes = lax.broadcasted_iota(jnp.int32, (8, TILE), 1)
    subs = lax.broadcasted_iota(jnp.int32, (8, TILE), 0)
    at = [subs == j for j in range(8)]
    a = list(rows)
    e = [jnp.where(lanes == subs + 8 * q, 1.0, 0.0).astype(F32) for q in range(16)]
    upper, inverse = [], []
    for p in range(16):
        ap, ep = a[p], e[p]
        c = [lane(ap, 8 * p + j) for j in range(8)]
        fa, fe, pivots = ap, ep, c[0]
        for j in range(8):
            pivot = sublane(c[j], j)
            scale = 1.0 / pivot
            cj = jnp.where(at[j], -1.0, c[j])
            if j:
                fa = jnp.where(at[j], ap, fa)
                fe = jnp.where(at[j], ep, fe)
                pivots = jnp.where(at[j], pivot, pivots)

            def step(x):
                return jnp.where(at[j], 0.0, x) - cj * (sublane(x, j) * scale)

            for k in range(j + 1, 8):
                c[k] = step(c[k])
            ap, ep = step(ap), step(ep)
        root = lax.rsqrt(pivots)
        upper.append(jnp.where(lanes >= subs + 8 * p, fa * root, 0.0))
        inverse.append(fe * root)
        wa = [sublane(ap, j) for j in range(8)]
        we = [sublane(ep, j) for j in range(8)]
        for q in range(p + 1, 16):
            cq = [lane(a[q], 8 * p + j) for j in range(8)]
            a[q] = a[q] - tree([cq[j] * wa[j] for j in range(8)])
            e[q] = e[q] - tree([cq[j] * we[j] for j in range(8)])
    return upper, inverse


def find(order_ref, wanted):
    place = jnp.int32(0)
    for t in range(32):
        place = place + (order_ref[t] == wanted).astype(jnp.int32) * t
    return jnp.minimum(place, 31)


def flag(condition):
    return condition.astype(jnp.int32).astype(F32)


def remote(src, dst, send, recv, row, col):
    return pltpu.make_async_remote_copy(
        src_ref=src,
        dst_ref=dst,
        send_sem=send,
        recv_sem=recv,
        device_id=(row, col),
        device_id_type=MESH,
    )


def each(count, skip, do):
    def turn(k, carry):
        @pl.when(k != skip)
        def _():
            do(k)

        return carry

    lax.fori_loop(0, count, turn, 0)


def kernel(
    pattern,
    row_order,
    col_order,
    matrix,
    out,
    staged,
    second,
    got0,
    got1,
    got23,
    zsend01,
    zsend2,
    zgot01,
    zgot2,
    pivot,
    work,
    ework,
    upper,
    inverse,
    cross,
    panels_own,
    panels_sib,
    shares,
    turned,
    scaled,
    a2a_send,
    got0_sem,
    got1_sem,
    got23_sem,
    z01_send,
    z01_recv,
    z2_send,
    z2_recv,
    piv_send,
    piv_recv,
    sib_send,
    sib_recv,
    p1_send,
    p1_recv,
    p2y_send,
    p2y_recv,
    p2x_send,
    p2x_recv,
    p3_send,
    p3_recv,
    c1_send,
    c1_recv,
    c2_send,
    c2_recv,
):
    row = lax.axis_index("row")
    col = lax.axis_index("col")
    chip, core = col // 2, col % 2
    y, x = chip // 4, chip % 4
    sibling = chip * 2 + (1 - core)

    barrier = pltpu.get_barrier_semaphore()

    def greet_col(k):
        pl.semaphore_signal(barrier, inc=1, device_id=(row, k), device_id_type=MESH)

    def greet_row(k):
        pl.semaphore_signal(barrier, inc=1, device_id=(k, col), device_id_type=MESH)

    each(32, col, greet_col)
    each(8, row, greet_row)

    place0, place1 = find(row_order, 0), find(row_order, 1)
    z0, z1 = place0 // 4, place1 // 4
    local0, local1 = place0 % 4, place1 % 4
    u0, u1 = find(col_order, 0), find(col_order, 1)
    same = (local0 == local1).astype(jnp.int32)
    step = (local1 - local0 + 4) % 4 + same
    order = [
        local0,
        (local0 + step) % 4,
        (local0 + 1 + (step == 1).astype(jnp.int32)) % 4,
        (local0 + 3 - (step == 3).astype(jnp.int32)) % 4,
    ]

    def stage(slot):
        staged[slot] = matrix[order[slot]]

    stage(0)
    pl.semaphore_wait(barrier, 31 + 7)

    def a2a(slot, got, got_sem, sends):
        def piece(k):
            return staged.at[slot, pl.ds(pl.multiple_of(k * CHUNK, 8), CHUNK)]

        def send(k):
            remote(
                piece(k), got.at[col], a2a_send.at[sends, k], got_sem.at[col], row, 2 * k
            ).start()

        each(16, jnp.where(core == 0, chip, 16), send)

        @pl.when(core == 0)
        def _():
            got[col] = staged[slot, pl.ds(pl.multiple_of(chip * CHUNK, 8), CHUNK), :]

    def a2a_wait(got, got_sem):
        def wait(k):
            remote(
                got.at[k], got.at[k], a2a_send.at[0, 0], got_sem.at[k], row, k
            ).wait_recv()

        each(32, col, wait)

    def a2a_sent(slot, sends):
        def wait(k):
            piece = staged.at[slot, pl.ds(pl.multiple_of(k * CHUNK, 8), CHUNK)]
            remote(
                piece, got0.at[col], a2a_send.at[sends, k], got0_sem.at[col], row, 2 * k
            ).wait_send()

        each(16, jnp.where(core == 0, chip, 16), wait)

    def piece23(k):
        return staged.at[pl.ds(2, 2), pl.ds(pl.multiple_of(k * CHUNK, 8), CHUNK)]

    def a2a23():
        def send(k):
            remote(
                piece23(k),
                got23.at[col],
                a2a_send.at[2, k],
                got23_sem.at[col],
                row,
                2 * k + 1,
            ).start()

        each(16, jnp.where(core == 1, chip, 16), send)

        @pl.when(core == 1)
        def _():
            got23[col] = staged[
                pl.ds(2, 2), pl.ds(pl.multiple_of(chip * CHUNK, 8), CHUNK), :
            ]

    def a2a23_sent():
        def wait(k):
            remote(
                piece23(k),
                got23.at[col],
                a2a_send.at[2, k],
                got23_sem.at[col],
                row,
                2 * k + 1,
            ).wait_send()

        each(16, jnp.where(core == 1, chip, 16), wait)

    def z_copy(src, got, send_sem, recv_sem, k):
        return remote(src, got.at[row], send_sem.at[k], recv_sem.at[row], k, col)

    def z_start(src, got, send_sem, recv_sem):
        each(8, row, lambda k: z_copy(src, got, send_sem, recv_sem, k).start())
        got[row] = src[...]

    def z_wait(src, got, send_sem, recv_sem):
        def wait(k):
            remote(
                src, got.at[k], send_sem.at[k], recv_sem.at[k], k, col
            ).wait_recv()

        each(8, row, wait)

    def z_sent(src, got, send_sem, recv_sem):
        each(8, row, lambda k: z_copy(src, got, send_sem, recv_sem, k).wait_send())

    def chunk_of(block, k):
        return pivot.at[block, pl.ds(pl.multiple_of(k * CHUNK, 8), CHUNK)]

    def piv_start(block):
        def send(k):
            remote(
                chunk_of(block, chip),
                chunk_of(block, chip),
                piv_send.at[block, k],
                piv_recv.at[block, chip],
                row,
                2 * k,
            ).start()

        each(16, chip, send)

    def piv_wait(block):
        def wait(k):
            remote(
                chunk_of(block, chip),
                chunk_of(block, k),
                piv_send.at[block, k],
                piv_recv.at[block, k],
                row,
                2 * k,
            ).wait_recv()

        each(16, chip, wait)

    def piv_sent(block):
        def wait(k):
            remote(
                chunk_of(block, chip),
                chunk_of(block, chip),
                piv_send.at[block, k],
                piv_recv.at[block, chip],
                row,
                2 * k,
            ).wait_send()

        each(16, chip, wait)

    def sib_copy(block):
        return remote(
            pivot.at[block],
            pivot.at[block],
            sib_send.at[block],
            sib_recv.at[block],
            row,
            sibling,
        )

    mine = pl.ds(pl.multiple_of(chip * CHUNK, 8), CHUNK)

    def panels_fill():
        @pl.when(core == 0)
        def _():
            for i, u in enumerate((u0, u1)):
                panels_own[i, 0, mine, :] = got0[u]
                panels_own[i, 1, mine, :] = got1[u]

        @pl.when(core == 1)
        def _():
            for i, u in enumerate((u0, u1)):
                panels_own[i, :, mine, :] = got23[u]

    def col_of(yy, xx):
        return (yy * 4 + xx) * 2 + core

    def p1_copy(i, k, at):
        there = col_of(y, k) if i == 0 else col_of(k, x)
        source = pl.ds(pl.multiple_of(at * CHUNK, 8), CHUNK)
        here = x if i == 0 else y
        return remote(
            panels_own.at[i, :, mine],
            panels_own.at[i, :, source],
            p1_send.at[i, k],
            p1_recv.at[i, here],
            row,
            there,
        )

    def p1_start():
        each(4, x, lambda k: p1_copy(0, k, chip).start())
        each(4, y, lambda k: p1_copy(1, k, chip).start())

    def p1_wait():
        def wait(i, k):
            at = y * 4 + k if i == 0 else k * 4 + x
            there = col_of(y, k) if i == 0 else col_of(k, x)
            source = pl.ds(pl.multiple_of(at * CHUNK, 8), CHUNK)
            remote(
                panels_own.at[i, :, mine],
                panels_own.at[i, :, source],
                p1_send.at[i, k],
                p1_recv.at[i, k],
                row,
                there,
            ).wait_recv()

        each(4, x, lambda k: wait(0, k))
        each(4, y, lambda k: wait(1, k))

    def p1_sent():
        each(4, x, lambda k: p1_copy(0, k, chip).wait_send())
        each(4, y, lambda k: p1_copy(1, k, chip).wait_send())

    def band(at):
        return panels_own.at[0, :, pl.ds(pl.multiple_of(at * 4 * CHUNK, 8), 4 * CHUNK)]

    def strip(yy, xx):
        return panels_own.at[
            1, :, pl.ds(pl.multiple_of((yy * 4 + xx) * CHUNK, 8), CHUNK)
        ]

    def p2_start():
        each(
            4,
            y,
            lambda k: remote(
                band(y), band(y), p2y_send.at[k], p2y_recv.at[y], row, col_of(k, x)
            ).start(),
        )

        def send(k):
            for yy in range(4):
                remote(
                    strip(yy, x),
                    strip(yy, x),
                    p2x_send.at[k, yy],
                    p2x_recv.at[x, yy],
                    row,
                    col_of(y, k),
                ).start()

        each(4, x, send)

    def p2_wait():
        each(
            4,
            y,
            lambda k: remote(
                band(y), band(k), p2y_send.at[k], p2y_recv.at[k], row, col_of(k, x)
            ).wait_recv(),
        )

        def wait(k):
            for yy in range(4):
                remote(
                    strip(yy, x),
                    strip(yy, k),
                    p2x_send.at[k, yy],
                    p2x_recv.at[k, yy],
                    row,
                    col_of(y, k),
                ).wait_recv()

        each(4, x, wait)

    def p2_sent():
        each(
            4,
            y,
            lambda k: remote(
                band(y), band(y), p2y_send.at[k], p2y_recv.at[y], row, col_of(k, x)
            ).wait_send(),
        )

        def wait(k):
            for yy in range(4):
                remote(
                    strip(yy, x),
                    strip(yy, x),
                    p2x_send.at[k, yy],
                    p2x_recv.at[x, yy],
                    row,
                    col_of(y, k),
                ).wait_send()

        each(4, x, wait)

    def p3_copy():
        return remote(panels_own, panels_sib, p3_send, p3_recv, row, sibling)

    def share(ref, i, k):
        return ref.at[i, pl.ds(pl.multiple_of(k * SHARE, 8), SHARE)]

    def c1_copy(i, k):
        src = staged.at[0] if i == 0 else second
        return remote(
            src.at[pl.ds(pl.multiple_of(k * SHARE, 8), SHARE)],
            shares.at[i, row],
            c1_send.at[i, k],
            c1_recv.at[i, row],
            k,
            col,
        )

    here = pl.ds(pl.multiple_of(row * SHARE, 8), SHARE)

    def c1_start():
        for i in range(2):
            each(8, row, lambda k: c1_copy(i, k).start())
        shares[0, row] = staged[0, here, :]
        shares[1, row] = second[here, :]

    def c1_wait():
        for i in range(2):
            each(
                8,
                row,
                lambda k: remote(
                    second.at[pl.ds(0, SHARE)],
                    shares.at[i, k],
                    c1_send.at[i, k],
                    c1_recv.at[i, k],
                    k,
                    col,
                ).wait_recv(),
            )

    def c1_sent():
        for i in range(2):
            each(8, row, lambda k: c1_copy(i, k).wait_send())

    def c2_copy(k, at):
        block = turned.at[:, pl.ds(pl.multiple_of(at * SHARE, 8), SHARE)]
        mine_ = turned.at[:, here]
        return mine_, block, k

    def c2_start():
        turned[0, here, :] = shares[0, z0]
        turned[1, here, :] = shares[1, z1]
        each(
            8,
            row,
            lambda k: remote(
                turned.at[:, here],
                turned.at[:, here],
                c2_send.at[k],
                c2_recv.at[row],
                k,
                col,
            ).start(),
        )

    def c2_wait():
        each(
            8,
            row,
            lambda k: remote(
                turned.at[:, here],
                turned.at[:, pl.ds(pl.multiple_of(k * SHARE, 8), SHARE)],
                c2_send.at[k],
                c2_recv.at[k],
                k,
                col,
            ).wait_recv(),
        )

    def c2_sent():
        each(
            8,
            row,
            lambda k: remote(
                turned.at[:, here],
                turned.at[:, here],
                c2_send.at[k],
                c2_recv.at[row],
                k,
                col,
            ).wait_send(),
        )

    a2a(0, got0, got0_sem, 0)
    stage(1)
    stage(2)
    stage(3)
    second[...] = staged[1 - same]
    upper[...] = jnp.zeros_like(upper)
    inverse[...] = jnp.zeros_like(inverse)
    ework[...] = jnp.zeros_like(ework)

    @pl.when(core == 0)
    def _():
        a2a_wait(got0, got0_sem)
        zsend01[0] = got0[u0]
        zsend01[1] = got0[u1]
        z_start(zsend01, zgot01, z01_send, z01_recv)
        z_wait(zsend01, zgot01, z01_send, z01_recv)
        pivot[0, mine, :] = zgot01[z0, 0]
        pivot[1, mine, :] = zgot01[z0, 1]
        piv_start(0)
        piv_start(1)
        piv_wait(0)
        sib_copy(0).start()

    @pl.when(core == 1)
    def _():
        sib_copy(0).wait_recv()

    a2a(1, got1, got1_sem, 1)
    c1_start()

    work[0] = pivot[0]

    def comm(b):
        @pl.when(b == 1)
        def _():
            @pl.when(core == 0)
            def _():
                piv_wait(1)
                sib_copy(1).start()
                a2a_wait(got1, got1_sem)
                weight = same.astype(F32)
                zsend2[...] = got0[u1] * weight + got1[u1] * (1.0 - weight)
                z_start(zsend2, zgot2, z2_send, z2_recv)

            a2a23()

        @pl.when(b == 2)
        def _():
            @pl.when(core == 0)
            def _():
                z_wait(zsend2, zgot2, z2_send, z2_recv)
                pivot[2, mine, :] = zgot2[z1]
                piv_start(2)

        @pl.when(b == 3)
        def _():
            @pl.when(core == 0)
            def _():
                piv_wait(2)
                sib_copy(2).start()

            @pl.when(core == 1)
            def _():
                a2a_wait(got23, got23_sem)

            panels_fill()
            p1_start()

            @pl.when(core == 1)
            def _():
                sib_copy(1).wait_recv()
                sib_copy(2).wait_recv()

            cross[...] = product(inverse[0], pivot[1], ROWS_COLS)
            work[1] = pivot[2] - product(cross[...], cross[...], COLS_COLS)

        @pl.when(b == 4)
        def _():
            p1_wait()
            p2_start()
            c1_wait()
            c2_start()

    def block_step(b, carry):
        comm(b)
        s = b // 3
        part = b % 3
        r0 = pl.multiple_of(part * TILE, TILE)
        tile = pl.ds(r0, TILE)
        rows = [
            work[s, pl.ds(pl.multiple_of(r0 + 8 * q, 8), 8), tile] for q in range(16)
        ]
        up, inv = factor_tile(rows)
        for q in range(16):
            at = pl.ds(pl.multiple_of(r0 + 8 * q, 8), 8)
            upper[s, at, tile] = up[q]
            inverse[s, at, tile] = inv[q]
        small = inverse[s, tile, tile]
        lanes = lax.broadcasted_iota(jnp.int32, (TILE, BLOCK), 1)
        after = lanes >= r0 + TILE
        before = lanes < r0
        down = jnp.where(after, product(small, work[s, tile, :], ROWS_COLS), 0.0)
        left = jnp.where(before, product(small, ework[s, tile, :], ROWS_COLS), 0.0)
        upper[s, tile, :] += down
        inverse[s, tile, :] += left

        @pl.when(part < 2)
        def _():
            work[s] -= product(down, down, COLS_COLS)
            ework[s] -= product(down, inverse[s, tile, :], COLS_COLS)

        return carry

    lax.fori_loop(0, 6, block_step, 0)

    j = col_order[col]
    mask0 = flag((pattern[j, 0] == 1) & (j > 0))
    mask1 = flag((pattern[j, 1] == 1) & (j > 1))
    is0, is1 = flag(j == 0), flag(j == 1)
    rest_of = flag(j > 1)
    c2_wait()
    v0 = split(inverse[0])
    v1 = split(inverse[1])
    cr = split(cross[...])
    r0 = product3(v0, split(turned[0] * mask0), ROWS_COLS)
    r0s = split(r0)
    r1 = product3(
        v1, split((turned[1] - product3(cr, r0s, COLS_COLS)) * mask1), ROWS_COLS
    )
    r1s = split(r1)
    p2_wait()
    p3_copy().start()

    place = [jnp.int32(0)] * 4
    for slot in range(4):
        for b in range(4):
            place[b] = place[b] + (order[slot] == b).astype(jnp.int32) * slot

    def update(half, ref):
        for k in range(2):
            first = 1 - half
            i = row_order[row * 4 + first * order[k] + half * order[2 + k]]
            m0 = flag((pattern[i, 0] == 1) & (i > 0))
            m1 = flag((pattern[i, 1] == 1) & (i > 1))
            s0 = product3(split(ref[0, k] * m0), v0, ROWS_ROWS)
            s0s = split(s0)
            rest = (ref[1, k] - product3(s0s, cr, ROWS_COLS)) * m1
            s1 = product3(split(rest), v1, ROWS_ROWS)
            change = product3(s0s, r0s, ROWS_COLS) + product3(
                split(s1), r1s, ROWS_COLS
            )
            scaled[half * 2 + k] = is0 * s0 + is1 * s1 - rest_of * change

    update(core, panels_own)
    p3_copy().wait_recv()
    update(1 - core, panels_sib)

    factors = [upper[s].T * flag(j == s) for s in range(2)]
    for b in range(4):
        i = row_order[row * 4 + b]
        keep = flag((pattern[i, j] == 1) & (i >= j))
        center0, center1 = flag((i == 0) & (j == 0)), flag((i == 1) & (j == 1))
        value = matrix[b] * rest_of + scaled[place[b]]
        out[b] = value * keep + factors[0] * center0 + factors[1] * center1

    a2a_sent(0, 0)
    a2a_sent(1, 1)
    a2a23_sent()
    p1_sent()
    p2_sent()
    p3_copy().wait_send()
    c1_sent()
    c2_sent()

    @pl.when(core == 0)
    def _():
        z_sent(zsend01, zgot01, z01_send, z01_recv)
        z_sent(zsend2, zgot2, z2_send, z2_recv)
        for block in range(3):
            piv_sent(block)
            sib_copy(block).wait_send()


def body(matrix, pattern, row_order, col_order):
    block = (BLOCK, BLOCK)
    vmem = lambda *shape: pltpu.VMEM(shape, F32)
    dma = lambda *shape: pltpu.SemaphoreType.DMA(shape)
    return pl.pallas_call(
        kernel,
        out_shape=jax.ShapeDtypeStruct((4, *block), F32),
        in_specs=[pl.BlockSpec(memory_space=pltpu.SMEM)] * 3
        + [pl.BlockSpec(memory_space=pltpu.VMEM)],
        out_specs=pl.BlockSpec(memory_space=pltpu.VMEM),
        scratch_shapes=[
            vmem(4, *block),
            vmem(*block),
            vmem(32, CHUNK, BLOCK),
            vmem(32, CHUNK, BLOCK),
            vmem(32, 2, CHUNK, BLOCK),
            vmem(2, CHUNK, BLOCK),
            vmem(CHUNK, BLOCK),
            vmem(8, 2, CHUNK, BLOCK),
            vmem(8, CHUNK, BLOCK),
            vmem(3, *block),
            vmem(2, *block),
            vmem(2, *block),
            vmem(2, *block),
            vmem(2, *block),
            vmem(*block),
            vmem(2, 2, *block),
            vmem(2, 2, *block),
            vmem(2, 8, SHARE, BLOCK),
            vmem(2, *block),
            vmem(4, *block),
            dma(3, 16),
            dma(32),
            dma(32),
            dma(32),
            dma(8),
            dma(8),
            dma(8),
            dma(8),
            dma(3, 16),
            dma(3, 16),
            dma(3),
            dma(3),
            dma(2, 4),
            dma(2, 4),
            dma(4),
            dma(4),
            dma(4, 4),
            dma(4, 4),
            pltpu.SemaphoreType.DMA,
            pltpu.SemaphoreType.DMA,
            dma(2, 8),
            dma(2, 8),
            dma(8),
            dma(8),
        ],
        compiler_params=pltpu.CompilerParams(
            collective_id=0, has_side_effects=True, vmem_limit_bytes=60 * 2**20
        ),
    )(pattern, row_order, col_order, matrix.reshape(4, *block)).reshape(matrix.shape)


def solution(mesh):
    in_specs = (P("row", "col"), P(), P(), P())
    out_specs = P("row", "col")
    return jax.shard_map(body, mesh=mesh, in_specs=in_specs, out_specs=out_specs, check_vma=False)
```

time: 741 us -> 142 us (0.19)
  the two profiles are of different devices: /device:TPU:1 before, /device:TPU:88 now
where the time goes in v1:
time: 142 us
  Pallas kernels  138 us (97%)
  local copies, waits for them, and re-layouts  3.22 us (2%)
    pallas_call x1, Pallas kernels, body(): pl.pallas_call(kernel, out_shape=jax.ShapeDtypeStruct((4, *block), F32),...  138 us
    unnamed x1, local copies, waits for them, and re-layouts  3.22 us

profile of v1, /device:TPU:88, one launch (start us, length us, event | category | flops | bytes accessed | tf_op | source)
XLA Modules:
  0.0 141.6 jit_solution(8666477988153812869)
XLA Ops:
  0.0 138.3 %shard_map.46 = f32[4,384,384]{2,1,0:T(8,128)} custom-call(s32[32,32]{1,0:T(8,128)} %pattern.1, s32[32]{0:T(128)} %row_order.1, s32[32]{0:T(128)} %col_order.1, f32[4,384,384]{2,1,0:T(8,128)} %bitcast.3), custom_call_target="tpu_custom_call" | custom-call | tf_op jit(solution)/shard_map/pallas_call | solution.py:757
  138.3 3.2 %copy.6 = f32[1536,384]{1,0:T(8,128)} copy(f32[1536,384]{1,0:T(8,128)} %bitcast.2) | data formatting | bytes 4718592

commit v2 on v1

--- a/solution.py
+++ b/solution.py
@@ -110,15 +110,9 @@
     )
 
 
-def each(count, skip, do):
-    def turn(k, carry):
-        @pl.when(k != skip)
-        def _():
-            do(k)
-
-        return carry
-
-    lax.fori_loop(0, count, turn, 0)
+def each(count, me, do):
+    for i in range(1, count):
+        do((me + i) % count)
 
 
 def kernel(
@@ -132,9 +126,11 @@
     got0,
     got1,
     got23,
-    zsend01,
+    zsend0,
+    zsend1,
     zsend2,
-    zgot01,
+    zgot0,
+    zgot1,
     zgot2,
     pivot,
     work,
@@ -151,8 +147,10 @@
     got0_sem,
     got1_sem,
     got23_sem,
-    z01_send,
-    z01_recv,
+    z0_send,
+    z0_recv,
+    z1_send,
+    z1_recv,
     z2_send,
     z2_recv,
     piv_send,
@@ -161,10 +159,8 @@
     sib_recv,
     p1_send,
     p1_recv,
-    p2y_send,
-    p2y_recv,
-    p2x_send,
-    p2x_recv,
+    p2_send,
+    p2_recv,
     p3_send,
     p3_recv,
     c1_send,
@@ -208,37 +204,45 @@
     stage(0)
     pl.semaphore_wait(barrier, 31 + 7)
 
+    def some(ref, count):
+        return ref.at[pl.ds(0, count)]
+
+    def arrived(ref, recv):
+        remote(ref, ref, p3_send, recv, row, sibling).wait_recv()
+
+    def left(ref, send):
+        remote(ref, ref, send, p3_recv, row, sibling).wait_send()
+
     def a2a(slot, got, got_sem, sends):
         def piece(k):
             return staged.at[slot, pl.ds(pl.multiple_of(k * CHUNK, 8), CHUNK)]
 
         def send(k):
             remote(
-                piece(k), got.at[col], a2a_send.at[sends, k], got_sem.at[col], row, 2 * k
+                piece(k), got.at[col], a2a_send.at[sends], got_sem, row, 2 * k
             ).start()
 
-        each(16, jnp.where(core == 0, chip, 16), send)
+        each(16, chip, send)
+
+        @pl.when(core == 1)
+        def _():
+            send(chip)
 
         @pl.when(core == 0)
         def _():
             got[col] = staged[slot, pl.ds(pl.multiple_of(chip * CHUNK, 8), CHUNK), :]
 
     def a2a_wait(got, got_sem):
-        def wait(k):
-            remote(
-                got.at[k], got.at[k], a2a_send.at[0, 0], got_sem.at[k], row, k
-            ).wait_recv()
-
-        each(32, col, wait)
-
-    def a2a_sent(slot, sends):
-        def wait(k):
-            piece = staged.at[slot, pl.ds(pl.multiple_of(k * CHUNK, 8), CHUNK)]
-            remote(
-                piece, got0.at[col], a2a_send.at[sends, k], got0_sem.at[col], row, 2 * k
-            ).wait_send()
-
-        each(16, jnp.where(core == 0, chip, 16), wait)
+        arrived(some(got, 31), got_sem)
+
+    def a2a_sent(sends):
+        @pl.when(core == 0)
+        def _():
+            left(some(got0, 15), a2a_send.at[sends])
+
+        @pl.when(core == 1)
+        def _():
+            left(some(got0, 16), a2a_send.at[sends])
 
     def piece23(k):
         return staged.at[pl.ds(2, 2), pl.ds(pl.multiple_of(k * CHUNK, 8), CHUNK)]
@@ -248,13 +252,17 @@
             remote(
                 piece23(k),
                 got23.at[col],
-                a2a_send.at[2, k],
-                got23_sem.at[col],
+                a2a_send.at[2],
+                got23_sem,
                 row,
                 2 * k + 1,
             ).start()
 
-        each(16, jnp.where(core == 1, chip, 16), send)
+        each(16, chip, send)
+
+        @pl.when(core == 0)
+        def _():
+            send(chip)
 
         @pl.when(core == 1)
         def _():
@@ -263,35 +271,27 @@
             ]
 
     def a2a23_sent():
-        def wait(k):
-            remote(
-                piece23(k),
-                got23.at[col],
-                a2a_send.at[2, k],
-                got23_sem.at[col],
-                row,
-                2 * k + 1,
-            ).wait_send()
-
-        each(16, jnp.where(core == 1, chip, 16), wait)
-
-    def z_copy(src, got, send_sem, recv_sem, k):
-        return remote(src, got.at[row], send_sem.at[k], recv_sem.at[row], k, col)
+        @pl.when(core == 0)
+        def _():
+            left(some(got23, 16), a2a_send.at[2])
+
+        @pl.when(core == 1)
+        def _():
+            left(some(got23, 15), a2a_send.at[2])
 
     def z_start(src, got, send_sem, recv_sem):
-        each(8, row, lambda k: z_copy(src, got, send_sem, recv_sem, k).start())
+        each(
+            8,
+            row,
+            lambda k: remote(src, got.at[row], send_sem, recv_sem, k, col).start(),
+        )
         got[row] = src[...]
 
     def z_wait(src, got, send_sem, recv_sem):
-        def wait(k):
-            remote(
-                src, got.at[k], send_sem.at[k], recv_sem.at[k], k, col
-            ).wait_recv()
-
-        each(8, row, wait)
+        arrived(some(got, 7), recv_sem)
 
     def z_sent(src, got, send_sem, recv_sem):
-        each(8, row, lambda k: z_copy(src, got, send_sem, recv_sem, k).wait_send())
+        left(some(got, 7), send_sem)
 
     def chunk_of(block, k):
         return pivot.at[block, pl.ds(pl.multiple_of(k * CHUNK, 8), CHUNK)]
@@ -301,8 +301,8 @@
             remote(
                 chunk_of(block, chip),
                 chunk_of(block, chip),
-                piv_send.at[block, k],
-                piv_recv.at[block, chip],
+                piv_send.at[block],
+                piv_recv.at[block],
                 row,
                 2 * k,
             ).start()
@@ -310,30 +310,10 @@
         each(16, chip, send)
 
     def piv_wait(block):
-        def wait(k):
-            remote(
-                chunk_of(block, chip),
-                chunk_of(block, k),
-                piv_send.at[block, k],
-                piv_recv.at[block, k],
-                row,
-                2 * k,
-            ).wait_recv()
-
-        each(16, chip, wait)
+        arrived(pivot.at[block, pl.ds(0, 15 * CHUNK)], piv_recv.at[block])
 
     def piv_sent(block):
-        def wait(k):
-            remote(
-                chunk_of(block, chip),
-                chunk_of(block, chip),
-                piv_send.at[block, k],
-                piv_recv.at[block, chip],
-                row,
-                2 * k,
-            ).wait_send()
-
-        each(16, chip, wait)
+        left(pivot.at[block, pl.ds(0, 15 * CHUNK)], piv_send.at[block])
 
     def sib_copy(block):
         return remote(
@@ -365,12 +345,11 @@
     def p1_copy(i, k, at):
         there = col_of(y, k) if i == 0 else col_of(k, x)
         source = pl.ds(pl.multiple_of(at * CHUNK, 8), CHUNK)
-        here = x if i == 0 else y
         return remote(
             panels_own.at[i, :, mine],
             panels_own.at[i, :, source],
-            p1_send.at[i, k],
-            p1_recv.at[i, here],
+            p1_send.at[i],
+            p1_recv.at[i],
             row,
             there,
         )
@@ -380,25 +359,12 @@
         each(4, y, lambda k: p1_copy(1, k, chip).start())
 
     def p1_wait():
-        def wait(i, k):
-            at = y * 4 + k if i == 0 else k * 4 + x
-            there = col_of(y, k) if i == 0 else col_of(k, x)
-            source = pl.ds(pl.multiple_of(at * CHUNK, 8), CHUNK)
-            remote(
-                panels_own.at[i, :, mine],
-                panels_own.at[i, :, source],
-                p1_send.at[i, k],
-                p1_recv.at[i, k],
-                row,
-                there,
-            ).wait_recv()
-
-        each(4, x, lambda k: wait(0, k))
-        each(4, y, lambda k: wait(1, k))
+        for i in range(2):
+            arrived(panels_own.at[i, :, pl.ds(0, 3 * CHUNK)], p1_recv.at[i])
 
     def p1_sent():
-        each(4, x, lambda k: p1_copy(0, k, chip).wait_send())
-        each(4, y, lambda k: p1_copy(1, k, chip).wait_send())
+        for i in range(2):
+            left(panels_own.at[i, :, pl.ds(0, 3 * CHUNK)], p1_send.at[i])
 
     def band(at):
         return panels_own.at[0, :, pl.ds(pl.multiple_of(at * 4 * CHUNK, 8), 4 * CHUNK)]
@@ -413,7 +379,7 @@
             4,
             y,
             lambda k: remote(
-                band(y), band(y), p2y_send.at[k], p2y_recv.at[y], row, col_of(k, x)
+                band(y), band(y), p2_send.at[0], p2_recv.at[0], row, col_of(k, x)
             ).start(),
         )
 
@@ -422,8 +388,8 @@
                 remote(
                     strip(yy, x),
                     strip(yy, x),
-                    p2x_send.at[k, yy],
-                    p2x_recv.at[x, yy],
+                    p2_send.at[1],
+                    p2_recv.at[1],
                     row,
                     col_of(y, k),
                 ).start()
@@ -431,48 +397,12 @@
         each(4, x, send)
 
     def p2_wait():
-        each(
-            4,
-            y,
-            lambda k: remote(
-                band(y), band(k), p2y_send.at[k], p2y_recv.at[k], row, col_of(k, x)
-            ).wait_recv(),
-        )
-
-        def wait(k):
-            for yy in range(4):
-                remote(
-                    strip(yy, x),
-                    strip(yy, k),
-                    p2x_send.at[k, yy],
-                    p2x_recv.at[k, yy],
-                    row,
-                    col_of(y, k),
-                ).wait_recv()
-
-        each(4, x, wait)
+        for i in range(2):
+            arrived(panels_own.at[i, :, pl.ds(0, 12 * CHUNK)], p2_recv.at[i])
 
     def p2_sent():
-        each(
-            4,
-            y,
-            lambda k: remote(
-                band(y), band(y), p2y_send.at[k], p2y_recv.at[y], row, col_of(k, x)
-            ).wait_send(),
-        )
-
-        def wait(k):
-            for yy in range(4):
-                remote(
-                    strip(yy, x),
-                    strip(yy, x),
-                    p2x_send.at[k, yy],
-                    p2x_recv.at[x, yy],
-                    row,
-                    col_of(y, k),
-                ).wait_send()
-
-        each(4, x, wait)
+        for i in range(2):
+            left(panels_own.at[i, :, pl.ds(0, 12 * CHUNK)], p2_send.at[i])
 
     def p3_copy():
         return remote(panels_own, panels_sib, p3_send, p3_recv, row, sibling)
@@ -485,8 +415,8 @@
         return remote(
             src.at[pl.ds(pl.multiple_of(k * SHARE, 8), SHARE)],
             shares.at[i, row],
-            c1_send.at[i, k],
-            c1_recv.at[i, row],
+            c1_send.at[i],
+            c1_recv.at[i],
             k,
             col,
         )
@@ -501,27 +431,11 @@
 
     def c1_wait():
         for i in range(2):
-            each(
-                8,
-                row,
-                lambda k: remote(
-                    second.at[pl.ds(0, SHARE)],
-                    shares.at[i, k],
-                    c1_send.at[i, k],
-                    c1_recv.at[i, k],
-                    k,
-                    col,
-                ).wait_recv(),
-            )
+            arrived(shares.at[i, pl.ds(0, 7)], c1_recv.at[i])
 
     def c1_sent():
         for i in range(2):
-            each(8, row, lambda k: c1_copy(i, k).wait_send())
-
-    def c2_copy(k, at):
-        block = turned.at[:, pl.ds(pl.multiple_of(at * SHARE, 8), SHARE)]
-        mine_ = turned.at[:, here]
-        return mine_, block, k
+            left(shares.at[i, pl.ds(0, 7)], c1_send.at[i])
 
     def c2_start():
         turned[0, here, :] = shares[0, z0]
@@ -532,46 +446,25 @@
             lambda k: remote(
                 turned.at[:, here],
                 turned.at[:, here],
-                c2_send.at[k],
-                c2_recv.at[row],
+                c2_send,
+                c2_recv,
                 k,
                 col,
             ).start(),
         )
 
     def c2_wait():
-        each(
-            8,
-            row,
-            lambda k: remote(
-                turned.at[:, here],
-                turned.at[:, pl.ds(pl.multiple_of(k * SHARE, 8), SHARE)],
-                c2_send.at[k],
-                c2_recv.at[k],
-                k,
-                col,
-            ).wait_recv(),
-        )
+        arrived(turned.at[:, pl.ds(0, 7 * SHARE)], c2_recv)
 
     def c2_sent():
-        each(
-            8,
-            row,
-            lambda k: remote(
-                turned.at[:, here],
-                turned.at[:, here],
-                c2_send.at[k],
-                c2_recv.at[row],
-                k,
-                col,
-            ).wait_send(),
-        )
+        left(turned.at[:, pl.ds(0, 7 * SHARE)], c2_send)
 
     a2a(0, got0, got0_sem, 0)
     stage(1)
     stage(2)
     stage(3)
     second[...] = staged[1 - same]
+    c1_start()
     upper[...] = jnp.zeros_like(upper)
     inverse[...] = jnp.zeros_like(inverse)
     ework[...] = jnp.zeros_like(ework)
@@ -579,14 +472,23 @@
     @pl.when(core == 0)
     def _():
         a2a_wait(got0, got0_sem)
-        zsend01[0] = got0[u0]
-        zsend01[1] = got0[u1]
-        z_start(zsend01, zgot01, z01_send, z01_recv)
-        z_wait(zsend01, zgot01, z01_send, z01_recv)
-        pivot[0, mine, :] = zgot01[z0, 0]
-        pivot[1, mine, :] = zgot01[z0, 1]
+        zsend0[...] = got0[u0]
+        z_start(zsend0, zgot0, z0_send, z0_recv)
+
+    a2a(1, got1, got1_sem, 1)
+
+    @pl.when(core == 0)
+    def _():
+        zsend1[...] = got0[u1]
+        z_wait(zsend0, zgot0, z0_send, z0_recv)
+        pivot[0, mine, :] = zgot0[z0]
         piv_start(0)
-        piv_start(1)
+        z_start(zsend1, zgot1, z1_send, z1_recv)
+
+    a2a23()
+
+    @pl.when(core == 0)
+    def _():
         piv_wait(0)
         sib_copy(0).start()
 
@@ -594,32 +496,42 @@
     def _():
         sib_copy(0).wait_recv()
 
-    a2a(1, got1, got1_sem, 1)
-    c1_start()
-
     work[0] = pivot[0]
 
     def comm(b):
         @pl.when(b == 1)
+        def _():
+            @pl.when(core == 0)
+            def _():
+                z_wait(zsend1, zgot1, z1_send, z1_recv)
+                pivot[1, mine, :] = zgot1[z0]
+                piv_start(1)
+                a2a_wait(got1, got1_sem)
+                weight = same.astype(F32)
+                zsend2[...] = got0[u1] * weight + got1[u1] * (1.0 - weight)
+                z_start(zsend2, zgot2, z2_send, z2_recv)
+
+            @pl.when(core == 1)
+            def _():
+                a2a_wait(got23, got23_sem)
+
+            panels_fill()
+            p1_start()
+
+        @pl.when(b == 2)
         def _():
             @pl.when(core == 0)
             def _():
                 piv_wait(1)
                 sib_copy(1).start()
-                a2a_wait(got1, got1_sem)
-                weight = same.astype(F32)
-                zsend2[...] = got0[u1] * weight + got1[u1] * (1.0 - weight)
-                z_start(zsend2, zgot2, z2_send, z2_recv)
-
-            a2a23()
-
-        @pl.when(b == 2)
-        def _():
-            @pl.when(core == 0)
-            def _():
                 z_wait(zsend2, zgot2, z2_send, z2_recv)
                 pivot[2, mine, :] = zgot2[z1]
                 piv_start(2)
+
+            p1_wait()
+            p2_start()
+            c1_wait()
+            c2_start()
 
         @pl.when(b == 3)
         def _():
@@ -630,25 +542,16 @@
 
             @pl.when(core == 1)
             def _():
-                a2a_wait(got23, got23_sem)
-
-            panels_fill()
-            p1_start()
-
-            @pl.when(core == 1)
-            def _():
                 sib_copy(1).wait_recv()
                 sib_copy(2).wait_recv()
 
             cross[...] = product(inverse[0], pivot[1], ROWS_COLS)
             work[1] = pivot[2] - product(cross[...], cross[...], COLS_COLS)
 
-        @pl.when(b == 4)
-        def _():
-            p1_wait()
-            p2_start()
-            c1_wait()
-            c2_start()
+        @pl.when(b == 5)
+        def _():
+            p2_wait()
+            p3_copy().start()
 
     def block_step(b, carry):
         comm(b)
@@ -669,9 +572,9 @@
         after = lanes >= r0 + TILE
         before = lanes < r0
         down = jnp.where(after, product(small, work[s, tile, :], ROWS_COLS), 0.0)
-        left = jnp.where(before, product(small, ework[s, tile, :], ROWS_COLS), 0.0)
+        behind = jnp.where(before, product(small, ework[s, tile, :], ROWS_COLS), 0.0)
         upper[s, tile, :] += down
-        inverse[s, tile, :] += left
+        inverse[s, tile, :] += behind
 
         @pl.when(part < 2)
         def _():
@@ -697,9 +600,6 @@
         v1, split((turned[1] - product3(cr, r0s, COLS_COLS)) * mask1), ROWS_COLS
     )
     r1s = split(r1)
-    p2_wait()
-    p3_copy().start()
-
     place = [jnp.int32(0)] * 4
     for slot in range(4):
         for b in range(4):
@@ -732,8 +632,8 @@
         value = matrix[b] * rest_of + scaled[place[b]]
         out[b] = value * keep + factors[0] * center0 + factors[1] * center1
 
-    a2a_sent(0, 0)
-    a2a_sent(1, 1)
+    a2a_sent(0)
+    a2a_sent(1)
     a2a23_sent()
     p1_sent()
     p2_sent()
@@ -743,7 +643,8 @@
 
     @pl.when(core == 0)
     def _():
-        z_sent(zsend01, zgot01, z01_send, z01_recv)
+        z_sent(zsend0, zgot0, z0_send, z0_recv)
+        z_sent(zsend1, zgot1, z1_send, z1_recv)
         z_sent(zsend2, zgot2, z2_send, z2_recv)
         for block in range(3):
             piv_sent(block)
@@ -766,9 +667,11 @@
             vmem(32, CHUNK, BLOCK),
             vmem(32, CHUNK, BLOCK),
             vmem(32, 2, CHUNK, BLOCK),
-            vmem(2, CHUNK, BLOCK),
             vmem(CHUNK, BLOCK),
-            vmem(8, 2, CHUNK, BLOCK),
+            vmem(CHUNK, BLOCK),
+            vmem(CHUNK, BLOCK),
+            vmem(8, CHUNK, BLOCK),
+            vmem(8, CHUNK, BLOCK),
             vmem(8, CHUNK, BLOCK),
             vmem(3, *block),
             vmem(2, *block),
@@ -781,30 +684,30 @@
             vmem(2, 8, SHARE, BLOCK),
             vmem(2, *block),
             vmem(4, *block),
-            dma(3, 16),
-            dma(32),
-            dma(32),
-            dma(32),
-            dma(8),
-            dma(8),
-            dma(8),
-            dma(8),
-            dma(3, 16),
-            dma(3, 16),
+            dma(3),
+            pltpu.SemaphoreType.DMA,
+            pltpu.SemaphoreType.DMA,
+            pltpu.SemaphoreType.DMA,
+            pltpu.SemaphoreType.DMA,
+            pltpu.SemaphoreType.DMA,
+            pltpu.SemaphoreType.DMA,
+            pltpu.SemaphoreType.DMA,
+            pltpu.SemaphoreType.DMA,
+            pltpu.SemaphoreType.DMA,
             dma(3),
             dma(3),
-            dma(2, 4),
-            dma(2, 4),
-            dma(4),
-            dma(4),
-            dma(4, 4),
-            dma(4, 4),
-            pltpu.SemaphoreType.DMA,
-            pltpu.SemaphoreType.DMA,
-            dma(2, 8),
-            dma(2, 8),
-            dma(8),
-            dma(8),
+            dma(3),
+            dma(3),
+            dma(2),
+            dma(2),
+            dma(2),
+            dma(2),
+            pltpu.SemaphoreType.DMA,
+            pltpu.SemaphoreType.DMA,
+            dma(2),
+            dma(2),
+            pltpu.SemaphoreType.DMA,
+            pltpu.SemaphoreType.DMA,
         ],
         compiler_params=pltpu.CompilerParams(
             collective_id=0, has_side_effects=True, vmem_limit_bytes=60 * 2**20

time: 142 us -> 121 us (0.85)
  the two profiles are of different devices: /device:TPU:88 before, /device:TPU:1 now
where the time goes in v2:
time: 121 us; the launch traced here: 119 us
  Pallas kernels  116 us (96%)
  local copies, waits for them, and re-layouts  3.22 us (3%)
    pallas_call x1, Pallas kernels, body(): pl.pallas_call(kernel, out_shape=jax.ShapeDtypeStruct((4, *block), F32),...  116 us
    unnamed x1, local copies, waits for them, and re-layouts  3.22 us

profile of v2, /device:TPU:1, one launch (start us, length us, event | category | flops | bytes accessed | tf_op | source)
XLA Modules:
  0.0 118.9 jit_solution(10912040008695735646)
XLA Ops:
  0.0 115.7 %shard_map.46 = f32[4,384,384]{2,1,0:T(8,128)} custom-call(s32[32,32]{1,0:T(8,128)} %pattern.1, s32[32]{0:T(128)} %row_order.1, s32[32]{0:T(128)} %col_order.1, f32[4,384,384]{2,1,0:T(8,128)} %bitcast.3), custom_call_target="tpu_custom_call" | custom-call | tf_op jit(solution)/shard_map/pallas_call | solution.py:658
  115.7 3.2 %copy.6 = f32[1536,384]{1,0:T(8,128)} copy(f32[1536,384]{1,0:T(8,128)} %bitcast.2) | data formatting | bytes 4718592

commit v3 on v2

--- a/solution.py
+++ b/solution.py
@@ -29,11 +29,17 @@
     return high, (value - high.astype(F32)).astype(BF16)
 
 
-def product3(left, right, over):
-    def part(a, b):
-        return lax.dot_general(a, b, (over, ((), ())), preferred_element_type=F32)
-
-    return part(left[0], right[0]) + (part(left[0], right[1]) + part(left[1], right[0]))
+def product3(pairs, over):
+    left, right = [], []
+    for a, b in pairs:
+        left += [a[0], a[0], a[1]]
+        right += [b[0], b[1], b[0]]
+    return lax.dot_general(
+        jnp.concatenate(left, axis=over[0][0]),
+        jnp.concatenate(right, axis=over[1][0]),
+        (over, ((), ())),
+        preferred_element_type=F32,
+    )
 
 
 def lane(value, k):
@@ -57,9 +63,14 @@
     a = list(rows)
     e = [jnp.where(lanes == subs + 8 * q, 1.0, 0.0).astype(F32) for q in range(16)]
     upper, inverse = [], []
+    c = [lane(a[0], j) for j in range(8)]
     for p in range(16):
         ap, ep = a[p], e[p]
-        c = [lane(ap, 8 * p + j) for j in range(8)]
+        ahead, beside, below = [], [], []
+        if p < 15:
+            ahead = [lane(ap, 8 * p + 8 + k) for k in range(8)]
+            beside = [lane(a[p + 1], 8 * p + j) for j in range(8)]
+            below = [lane(a[p + 1], 8 * p + 8 + k) for k in range(8)]
         fa, fe, pivots = ap, ep, c[0]
         for j in range(8):
             pivot = sublane(c[j], j)
@@ -75,14 +86,19 @@
 
             for k in range(j + 1, 8):
                 c[k] = step(c[k])
+            ahead = [step(x) for x in ahead]
             ap, ep = step(ap), step(ep)
+        c = [
+            below[k] - tree([beside[j] * sublane(ahead[k], j) for j in range(8)])
+            for k in range(len(ahead))
+        ]
         root = lax.rsqrt(pivots)
         upper.append(jnp.where(lanes >= subs + 8 * p, fa * root, 0.0))
         inverse.append(fe * root)
         wa = [sublane(ap, j) for j in range(8)]
         we = [sublane(ep, j) for j in range(8)]
         for q in range(p + 1, 16):
-            cq = [lane(a[q], 8 * p + j) for j in range(8)]
+            cq = beside if q == p + 1 else [lane(a[q], 8 * p + j) for j in range(8)]
             a[q] = a[q] - tree([cq[j] * wa[j] for j in range(8)])
             e[q] = e[q] - tree([cq[j] * we[j] for j in range(8)])
     return upper, inverse
@@ -423,11 +439,9 @@
 
     here = pl.ds(pl.multiple_of(row * SHARE, 8), SHARE)
 
-    def c1_start():
-        for i in range(2):
-            each(8, row, lambda k: c1_copy(i, k).start())
-        shares[0, row] = staged[0, here, :]
-        shares[1, row] = second[here, :]
+    def c1_start(i):
+        each(8, row, lambda k: c1_copy(i, k).start())
+        shares[i, row] = staged[0, here, :] if i == 0 else second[here, :]
 
     def c1_wait():
         for i in range(2):
@@ -464,7 +478,12 @@
     stage(2)
     stage(3)
     second[...] = staged[1 - same]
-    c1_start()
+    c1_start(0)
+
+    @pl.when(core == 1)
+    def _():
+        c1_start(1)
+
     upper[...] = jnp.zeros_like(upper)
     inverse[...] = jnp.zeros_like(inverse)
     ework[...] = jnp.zeros_like(ework)
@@ -484,6 +503,7 @@
         pivot[0, mine, :] = zgot0[z0]
         piv_start(0)
         z_start(zsend1, zgot1, z1_send, z1_recv)
+        c1_start(1)
 
     a2a23()
 
@@ -511,13 +531,6 @@
                 zsend2[...] = got0[u1] * weight + got1[u1] * (1.0 - weight)
                 z_start(zsend2, zgot2, z2_send, z2_recv)
 
-            @pl.when(core == 1)
-            def _():
-                a2a_wait(got23, got23_sem)
-
-            panels_fill()
-            p1_start()
-
         @pl.when(b == 2)
         def _():
             @pl.when(core == 0)
@@ -528,8 +541,12 @@
                 pivot[2, mine, :] = zgot2[z1]
                 piv_start(2)
 
-            p1_wait()
-            p2_start()
+            @pl.when(core == 1)
+            def _():
+                a2a_wait(got23, got23_sem)
+
+            panels_fill()
+            p1_start()
             c1_wait()
             c2_start()
 
@@ -545,13 +562,10 @@
                 sib_copy(1).wait_recv()
                 sib_copy(2).wait_recv()
 
+            p1_wait()
+            p2_start()
             cross[...] = product(inverse[0], pivot[1], ROWS_COLS)
             work[1] = pivot[2] - product(cross[...], cross[...], COLS_COLS)
-
-        @pl.when(b == 5)
-        def _():
-            p2_wait()
-            p3_copy().start()
 
     def block_step(b, carry):
         comm(b)
@@ -590,46 +604,46 @@
     mask1 = flag((pattern[j, 1] == 1) & (j > 1))
     is0, is1 = flag(j == 0), flag(j == 1)
     rest_of = flag(j > 1)
-    c2_wait()
     v0 = split(inverse[0])
     v1 = split(inverse[1])
     cr = split(cross[...])
-    r0 = product3(v0, split(turned[0] * mask0), ROWS_COLS)
-    r0s = split(r0)
-    r1 = product3(
-        v1, split((turned[1] - product3(cr, r0s, COLS_COLS)) * mask1), ROWS_COLS
-    )
-    r1s = split(r1)
+
     place = [jnp.int32(0)] * 4
     for slot in range(4):
         for b in range(4):
             place[b] = place[b] + (order[slot] == b).astype(jnp.int32) * slot
 
-    def update(half, ref):
+    def scale(half, ref):
         for k in range(2):
             first = 1 - half
             i = row_order[row * 4 + first * order[k] + half * order[2 + k]]
             m0 = flag((pattern[i, 0] == 1) & (i > 0))
             m1 = flag((pattern[i, 1] == 1) & (i > 1))
-            s0 = product3(split(ref[0, k] * m0), v0, ROWS_ROWS)
-            s0s = split(s0)
-            rest = (ref[1, k] - product3(s0s, cr, ROWS_COLS)) * m1
-            s1 = product3(split(rest), v1, ROWS_ROWS)
-            change = product3(s0s, r0s, ROWS_COLS) + product3(
-                split(s1), r1s, ROWS_COLS
-            )
-            scaled[half * 2 + k] = is0 * s0 + is1 * s1 - rest_of * change
-
-    update(core, panels_own)
+            s0 = product3([(split(ref[0, k] * m0), v0)], ROWS_ROWS)
+            rest = (ref[1, k] - product3([(split(s0), cr)], ROWS_COLS)) * m1
+            scaled[half * 2 + k, 0] = s0
+            scaled[half * 2 + k, 1] = product3([(split(rest), v1)], ROWS_ROWS)
+
+    p2_wait()
+    p3_copy().start()
+    scale(core, panels_own)
     p3_copy().wait_recv()
-    update(1 - core, panels_sib)
+    scale(1 - core, panels_sib)
+
+    c2_wait()
+    r0 = product3([(v0, split(turned[0] * mask0))], ROWS_COLS)
+    r0s = split(r0)
+    rest = (turned[1] - product3([(cr, r0s)], COLS_COLS)) * mask1
+    r1s = split(product3([(v1, split(rest))], ROWS_COLS))
 
     factors = [upper[s].T * flag(j == s) for s in range(2)]
     for b in range(4):
         i = row_order[row * 4 + b]
         keep = flag((pattern[i, j] == 1) & (i >= j))
         center0, center1 = flag((i == 0) & (j == 0)), flag((i == 1) & (j == 1))
-        value = matrix[b] * rest_of + scaled[place[b]]
+        s0, s1 = scaled[place[b], 0], scaled[place[b], 1]
+        change = product3([(split(s0), r0s), (split(s1), r1s)], ROWS_COLS)
+        value = (matrix[b] - change) * rest_of + s0 * is0 + s1 * is1
         out[b] = value * keep + factors[0] * center0 + factors[1] * center1
 
     a2a_sent(0)
@@ -683,7 +697,7 @@
             vmem(2, 2, *block),
             vmem(2, 8, SHARE, BLOCK),
             vmem(2, *block),
-            vmem(4, *block),
+            vmem(4, 2, *block),
             dma(3),
             pltpu.SemaphoreType.DMA,
             pltpu.SemaphoreType.DMA,

time: 121 us -> 102 us (0.84); the launches traced: 119 us -> 102 us
  Pallas kernels: 116 us -> 99.1 us
    pallas_call x1, Pallas kernels: 116 us -> 99.1 us  [body(): pl.pallas_call(kernel, out_shape=jax.ShapeDtypeStruct((4, *block), F32),...]
where the time goes in v3:
time: 102 us
  Pallas kernels  99.1 us (97%)
  local copies, waits for them, and re-layouts  3.22 us (3%)
    pallas_call x1, Pallas kernels, body(): pl.pallas_call(kernel, out_shape=jax.ShapeDtypeStruct((4, *block), F32),...  99.1 us
    unnamed x1, local copies, waits for them, and re-layouts  3.22 us

profile of v3, /device:TPU:1, one launch (start us, length us, event | category | flops | bytes accessed | tf_op | source)
XLA Modules:
  0.0 102.3 jit_solution(14907784304670355423)
XLA Ops:
  0.0 99.1 %shard_map.46 = f32[4,384,384]{2,1,0:T(8,128)} custom-call(s32[32,32]{1,0:T(8,128)} %pattern.1, s32[32]{0:T(128)} %row_order.1, s32[32]{0:T(128)} %col_order.1, f32[4,384,384]{2,1,0:T(8,128)} %bitcast.3), custom_call_target="tpu_custom_call" | custom-call | tf_op jit(solution)/shard_map/pallas_call | solution.py:672
  99.1 3.2 %copy.6 = f32[1536,384]{1,0:T(8,128)} copy(f32[1536,384]{1,0:T(8,128)} %bitcast.2) | data formatting | bytes 4718592

commit v4 on v3

--- a/solution.py
+++ b/solution.py
@@ -479,11 +479,6 @@
     stage(3)
     second[...] = staged[1 - same]
     c1_start(0)
-
-    @pl.when(core == 1)
-    def _():
-        c1_start(1)
-
     upper[...] = jnp.zeros_like(upper)
     inverse[...] = jnp.zeros_like(inverse)
     ework[...] = jnp.zeros_like(ework)
@@ -515,6 +510,7 @@
     @pl.when(core == 1)
     def _():
         sib_copy(0).wait_recv()
+        c1_start(1)
 
     work[0] = pivot[0]
 

time: 102 us -> 101 us (level)
  Pallas kernels: 99.1 us -> 97.9 us
    pallas_call x1, Pallas kernels: 99.1 us -> 97.9 us  [body(): pl.pallas_call(kernel, out_shape=jax.ShapeDtypeStruct((4, *block), F32),...]
where the time goes in v4:
time: 101 us
  Pallas kernels  97.9 us (97%)
  local copies, waits for them, and re-layouts  3.22 us (3%)
    pallas_call x1, Pallas kernels, body(): pl.pallas_call(kernel, out_shape=jax.ShapeDtypeStruct((4, *block), F32),...  97.9 us
    unnamed x1, local copies, waits for them, and re-layouts  3.22 us

profile of v4, /device:TPU:1, one launch (start us, length us, event | category | flops | bytes accessed | tf_op | source)
XLA Modules:
  0.0 101.1 jit_solution(132099522530145235)
XLA Ops:
  0.0 97.9 %shard_map.46 = f32[4,384,384]{2,1,0:T(8,128)} custom-call(s32[32,32]{1,0:T(8,128)} %pattern.1, s32[32]{0:T(128)} %row_order.1, s32[32]{0:T(128)} %col_order.1, f32[4,384,384]{2,1,0:T(8,128)} %bitcast.3), custom_call_target="tpu_custom_call" | custom-call | tf_op jit(solution)/shard_map/pallas_call | solution.py:668
  97.9 3.2 %copy.6 = f32[1536,384]{1,0:T(8,128)} copy(f32[1536,384]{1,0:T(8,128)} %bitcast.2) | data formatting | bytes 4718592

commit v5 on v4

--- a/solution.py
+++ b/solution.py
@@ -135,8 +135,12 @@
     pattern,
     row_order,
     col_order,
+    matrix_hbm,
+    out_hbm,
     matrix,
     out,
+    load_sem,
+    store_sem,
     staged,
     second,
     got0,
@@ -200,6 +204,8 @@
 
     each(32, col, greet_col)
     each(8, row, greet_row)
+    load = pltpu.make_async_copy(matrix_hbm, matrix, load_sem)
+    load.start()
 
     place0, place1 = find(row_order, 0), find(row_order, 1)
     z0, z1 = place0 // 4, place1 // 4
@@ -217,6 +223,7 @@
     def stage(slot):
         staged[slot] = matrix[order[slot]]
 
+    load.wait()
     stage(0)
     pl.semaphore_wait(barrier, 31 + 7)
 
@@ -641,7 +648,10 @@
         change = product3([(split(s0), r0s), (split(s1), r1s)], ROWS_COLS)
         value = (matrix[b] - change) * rest_of + s0 * is0 + s1 * is1
         out[b] = value * keep + factors[0] * center0 + factors[1] * center1
-
+        pltpu.make_async_copy(out.at[b], out_hbm.at[b], store_sem.at[b]).start()
+
+    for b in range(4):
+        pltpu.make_async_copy(out.at[b], out_hbm.at[b], store_sem.at[b]).wait()
     a2a_sent(0)
     a2a_sent(1)
     a2a23_sent()
@@ -669,9 +679,13 @@
         kernel,
         out_shape=jax.ShapeDtypeStruct((4, *block), F32),
         in_specs=[pl.BlockSpec(memory_space=pltpu.SMEM)] * 3
-        + [pl.BlockSpec(memory_space=pltpu.VMEM)],
-        out_specs=pl.BlockSpec(memory_space=pltpu.VMEM),
+        + [pl.BlockSpec(memory_space=pl.ANY)],
+        out_specs=pl.BlockSpec(memory_space=pl.ANY),
         scratch_shapes=[
+            vmem(4, *block),
+            vmem(4, *block),
+            pltpu.SemaphoreType.DMA,
+            dma(4),
             vmem(4, *block),
             vmem(*block),
             vmem(32, CHUNK, BLOCK),

time: 101 us -> 100 us (0.990)
  Pallas kernels: 97.9 us -> 96.6 us
    pallas_call x1, Pallas kernels: 97.9 us -> 96.6 us  [body(): pl.pallas_call(kernel, out_shape=jax.ShapeDtypeStruct((4, *block), F32),...]
where the time goes in v5:
time: 100 us; the launch traced here: 99.8 us
  Pallas kernels  96.6 us (97%)
  local copies, waits for them, and re-layouts  3.22 us (3%)
    pallas_call x1, Pallas kernels, body(): pl.pallas_call(kernel, out_shape=jax.ShapeDtypeStruct((4, *block), F32),...  96.6 us
    unnamed x1, local copies, waits for them, and re-layouts  3.22 us

profile of v5, /device:TPU:1, one launch (start us, length us, event | category | flops | bytes accessed | tf_op | source)
XLA Modules:
  0.0 99.8 jit_solution(15501911472590365365)
XLA Ops:
  0.0 96.6 %shard_map.46 = f32[4,384,384]{2,1,0:T(8,128)} custom-call(s32[32,32]{1,0:T(8,128)} %pattern.1, s32[32]{0:T(128)} %row_order.1, s32[32]{0:T(128)} %col_order.1, f32[4,384,384]{2,1,0:T(8,128)} %bitcast.3), custom_call_target="tpu_custom_call" | custom-call | tf_op jit(solution)/shard_map/pallas_call | solution.py:678
  96.6 3.2 %copy.6 = f32[1536,384]{1,0:T(8,128)} copy(f32[1536,384]{1,0:T(8,128)} %bitcast.2) | data formatting | bytes 4718592
